TPU v7x, 32 devices: a whole 2x2x4 slice. The times are simulated.
32 devices in a mesh: mol: 2 (over y), vir: 16 (over z, x, core), occ: 1.
Axes of the slice: x: 2, y: 2, z: 4, core: 2. Of those that a mesh axis runs over, the one named last changes fastest.
Arguments:
- amplitudes: float32 [384, 16384], P(('mol', 'occ'), 'vir'), parts along dimension 0, may hold values from -6 to 6
- ladder_ints: float32 [49152, 1536], P(('mol', 'vir')), parts along dimension 0, may hold values from -0.15625 to 0.15625
- hole_ints: float32 [384, 192], P('mol', 'occ'), parts along dimension 0, may hold values from -0.4375 to 0.4375
- sector_sizes: int32 [16], replicated, may hold values from 1 to 12, 128 in all
- device_perm: int32 [16], replicated, may hold values from 0 to 15, each once
- block_shift: int32 [16], replicated, may hold values from 0 to 7
Outputs:
- residual: float32 [384, 16384], P(('mol', 'occ'), 'vir'), parts along dimension 0
There are 2 independent parts, one for each index of `mol`. A program takes and returns all parts, laid end to end along the dimension named above; an argument that names none is the same for every part. Nothing has to cross between parts.
Inputs may be any that keep to these rules, and one draw needn't show every extreme that they name: `sector_sizes`: at least one sector has exactly 12 blocks; the sizes add up to 128.
All inputs are finite; a program needn't handle non-finite values.
Results may differ from a plain program's by a relative error of at most 0.0001.
Values sent between devices are 32-bit elements; how exact they have to be, the bound alone decides.
A program may use at most 128 MiB of HBM per device.

v0:
```python
import jax
import jax.numpy as jnp
from jax import lax
from jax.sharding import PartitionSpec as P

BLOCK = 128


def select_sum(mask, values):
    return jnp.sum(jnp.where(mask, values[None, :], 0), axis=1)


def tables(sector_sizes, device_perm, block_shift, vir_count, per_device):
    block_count = per_device * vir_count
    slot_ids = jnp.arange(block_count, dtype=jnp.int32)
    devices = jnp.arange(vir_count, dtype=jnp.int32)
    sector_ends = jnp.cumsum(sector_sizes)
    sector_starts = sector_ends - sector_sizes
    sector = jnp.sum((sector_ends[None, :] <= slot_ids[:, None]).astype(jnp.int32), axis=1)
    in_sector = sector[:, None] == devices[None, :]
    sector_rank = slot_ids - select_sum(in_sector, sector_starts)
    column = slot_ids % vir_count
    owner_dev = select_sum(column[:, None] == devices[None, :], device_perm)
    shift_of = select_sum(owner_dev[:, None] == devices[None, :], block_shift)
    local_idx = (slot_ids // vir_count + shift_of) % per_device
    return (sector, sector_rank, owner_dev, local_idx)


def send_back(
    ladder_out, sector, sector_rank, owner_dev, local_idx, my_index, vir_count, per_device
):
    devices = jnp.arange(vir_count, dtype=jnp.int32)
    mine = sector == my_index
    to_owner = mine[None, :] & (owner_dev[None, :] == devices[:, None])
    back_rank = select_sum(to_owner, sector_rank)
    back_live = jnp.any(to_owner, axis=1)
    outgoing = jnp.where(back_live[None, :, None], jnp.take(ladder_out, back_rank, axis=1), 0.0)
    returned = lax.all_to_all(outgoing, "vir", split_axis=1, concat_axis=1, tiled=True)
    local_ids = jnp.arange(per_device, dtype=jnp.int32)
    owned = owner_dev == my_index
    sector_of_local = select_sum(
        owned[None, :] & (local_idx[None, :] == local_ids[:, None]), sector
    )
    placed = jnp.take(returned, sector_of_local, axis=1)
    return placed.reshape(placed.shape[0], per_device * BLOCK)


def body(amplitudes, ladder_ints, hole_ints, sector_sizes, device_perm, block_shift):
    vir_count = lax.axis_size("vir")
    my_index = lax.axis_index("vir")
    rows_here = amplitudes.shape[0]
    per_device = amplitudes.shape[1] // BLOCK
    span = ladder_ints.shape[0] // BLOCK
    sector, sector_rank, owner_dev, local_idx = tables(
        sector_sizes, device_perm, block_shift, vir_count, per_device
    )
    blocks = amplitudes.reshape(rows_here, per_device, BLOCK)
    mine = sector == my_index
    rank_ids = jnp.arange(span, dtype=jnp.int32)
    global_ids = owner_dev * per_device + local_idx
    rank_hits = (mine[None, :] & (sector_rank[None, :] == rank_ids[:, None])).astype(jnp.float32)
    piece = lax.all_gather(blocks, "vir", axis=1, tiled=True)
    piece_ids = jnp.arange(piece.shape[1], dtype=jnp.int32)
    block_hits = (global_ids[:, None] == piece_ids[None, :]).astype(jnp.float32)
    onehot = jnp.dot(rank_hits, block_hits, precision=lax.Precision.HIGHEST)
    collected = jnp.einsum("rn,onx->orx", onehot, piece, precision=lax.Precision.HIGHEST)
    product = jnp.dot(
        collected.reshape(rows_here, span * BLOCK), ladder_ints, precision=lax.Precision.HIGHEST
    )
    particle = send_back(
        product.reshape(rows_here, span, BLOCK),
        sector,
        sector_rank,
        owner_dev,
        local_idx,
        my_index,
        vir_count,
        per_device,
    )
    partial_sum = jnp.dot(hole_ints, amplitudes, precision=lax.Precision.HIGHEST)
    summed = lax.psum(partial_sum, "occ")
    hole = lax.dynamic_slice_in_dim(summed, lax.axis_index("occ") * rows_here, rows_here, 0)
    return particle + hole


def solution(mesh):
    in_specs = (P(("mol", "occ"), "vir"), P(("mol", "vir"), None), P("mol", "occ"), P(), P(), P())
    out_specs = P(("mol", "occ"), "vir")
    return jax.shard_map(body, mesh=mesh, in_specs=in_specs, out_specs=out_specs, check_vma=False)
```

profile of v0, /device:TPU:0, one launch (start us, length us, event | category | flops | bytes accessed | tf_op | source)
XLA Modules:
  0.0 183.9 jit_solution(11997664336231446413)
XLA Ops:
  6.5 0.0 copy-start
  6.5 0.0 copy-start.2
  6.5 0.0 all-gather.2.cloned.1.call-start
  6.5 2.2 %copy.16 = f32[24,8,8,128]{3,2,1,0:T(8,128)} copy(f32[24,8,8,128]{3,1,2,0:T(8,128)} %bitcast.38) | data formatting | bytes 1572864
  8.7 0.0 all-gather.2.cloned.1.call-update
  8.8 0.0 copy-done.2
  8.8 0.1 copy.12
  8.9 0.1 reduce
  9.0 0.0 copy-start.3
  9.0 0.0 copy-start.4
  9.1 9.6 %copy.13 = f32[1536,1536]{0,1:T(8,128)} copy(f32[1536,1536]{1,0:T(8,128)} %param.7) | data formatting | bytes 18874368 | tf_op args[1]
  18.7 0.1 convert_reduce_fusion
  18.8 0.0 copy-done.3
  18.8 0.1 select_reduce_fusion.3
  18.9 0.1 select_reduce_fusion.1
  19.0 0.1 select_reduce_fusion
  19.1 0.1 fusion.2
  19.2 0.0 copy-done.4
  19.2 0.1 select_reduce_fusion.2
  19.3 0.2 convolution_bitcast_fusion.1
  19.5 96.8 %all-gather.2.cloned.1.call-done = f32[192,128,128]{2,1,0:T(8,128)} async-done(((f32[192,8,128]{2,1,0:T(8,128)}), f32[192,128,128]{2,1,0:T(8,128)}) %all-gather.2.cloned.1.call-update) | async-done | bytes 12582928 | tf_op jit(solution)/shard_map/all_gather | solution.py:62
  116.3 8.5 %convolution_bitcast_fusion = f32[192,12,128]{2,1,0:T(8,128)S(1)} fusion(f32[12,128,1]{1,0,2:T(8,128)S(1)} %convolution_bitcast_fusion.1, f32[192,128,128]{2,1,0:T(8,128)} %all-gather.2.cloned.1.call-done), kind=kOutput, calls=%fused_computation.3 | convolution fusion | flops 452984832 | bytes 13768704 | tf_op jit(solution)/shard_map/rn,onx->orx/dot_general | solution.py:66
  124.8 0.2 reshape.178
  125.0 12.0 %fusion.12 = f32[192,12,128]{2,0,1:T(8,128)S(1)} fusion(f32[192,1536,1]{1,0,2:T(8,128)S(1)} %reshape.178, f32[12,128,1536]{2,1,0:T(8,128)} %bitcast.36), kind=kOutput, calls=%fused_computation.53 | convolution fusion | flops 5435817984 | bytes 11796480 | tf_op jit(solution)/shard_map/dot_general | solution.py:67
  137.0 0.7 gather_fusion
  137.6 1.4 select_bitcast_fusion
  139.1 3.7 %all-to-all-start = ((f32[192,16,128]{2,0,1:T(8,128)}), f32[192,16,128]{2,0,1:T(8,128)S(1)}, u32[]{:S(2)}, u32[]{:S(2)}) async-start(f32[192,16,128]{2,0,1:T(8,128)} %select_bitcast_fusion), calls=%async_computation | async-start | bytes 3145728 | tf_op jit(solution)/shard_map/all_to_all | solution.py:38
  142.8 0.0 copy-start.1
  142.8 0.1 select_reduce_fusion.4
  143.0 0.1 broadcast_bitcast_fusion
  143.0 31.7 %all-to-all-done = f32[192,16,128]{2,0,1:T(8,128)S(1)} async-done(((f32[192,16,128]{2,0,1:T(8,128)}), f32[192,16,128]{2,0,1:T(8,128)S(1)}, u32[]{:S(2)}, u32[]{:S(2)}) %all-to-all-start) | async-done | bytes 1572896 | tf_op jit(solution)/shard_map/all_to_all | solution.py:38
  174.7 0.6 gather_fusion.1
  175.3 0.0 copy-done
  175.3 0.0 copy-done.1
  175.3 1.7 convolution_add_fusion
  (13 shorter events, 0.1 us)
Async XLA Ops:
  6.5 168.8 %copy-start = (f32[192,192]{1,0:T(8,128)S(1)}, f32[192,192]{1,0:T(8,128)}, u32[]{:S(2)}) copy-start(f32[192,192]{1,0:T(8,128)} %param.8) | copy-start | bytes 442372
  6.5 2.2 %copy-start.2 = (s32[16]{0:T(128)S(1)}, s32[16]{0:T(128)}, u32[]{:S(2)}) copy-start(s32[16]{0:T(128)} %param.9) | copy-start | bytes 196
  6.5 109.7 %all-gather.2.cloned.1.call-start = ((), (), s32[]{:S(2)}) async-start(), calls=%async_computation.1 | async-start | bytes 13369344 | tf_op jit(solution)/shard_map/all_gather | solution.py:62
  9.0 9.7 %copy-start.3 = (s32[16]{0:T(128)S(1)}, s32[16]{0:T(128)}, u32[]{:S(2)}) copy-start(s32[16]{0:T(128)} %param.10) | copy-start | bytes 196
  9.0 10.2 %copy-start.4 = (s32[16]{0:T(128)S(1)}, s32[16]{0:T(128)}, u32[]{:S(2)}) copy-start(s32[16]{0:T(128)} %param.11) | copy-start | bytes 196
  139.1 35.6 %all-to-all-start = ((f32[192,16,128]{2,0,1:T(8,128)}), f32[192,16,128]{2,0,1:T(8,128)S(1)}, u32[]{:S(2)}, u32[]{:S(2)}) async-start(f32[192,16,128]{2,0,1:T(8,128)} %select_bitcast_fusion), calls=%async_computation | async-start | bytes 3145728 | tf_op jit(solution)/shard_map/all_to_all | solution.py:38
  142.8 32.5 %copy-start.1 = (f32[192,1024]{1,0:T(8,128)S(1)}, f32[192,1024]{1,0:T(8,128)}, u32[]{:S(2)}) copy-start(f32[192,1024]{1,0:T(8,128)} %param.6) | copy-start | bytes 2359300
Sparse Core Ops, SparseCore 0:
  9.5 106.7 all-gather.1
where the time goes:
time: 188 us; the launch traced here: 184 us
  waiting for transfers between devices  128 us (68%)
  matrix products  22.4 us (12%)
  between operations  13.5 us (7%)
  local copies, waits for them, and re-layouts  13.4 us (7%)
  starting transfers between devices  3.71 us (2%)
  other arithmetic  2.37 us (1%)
    all_gather x1, waiting for transfers between devices, body(): piece = lax.all_gather(blocks, 'vir', axis=1, tiled=True)  96.8 us
    all_to_all x1, waiting for transfers between devices, send_back(): lax.all_to_all(outgoing, 'vir', split_axis=1, concat_axis=1, tiled=True)  31.7 us
    dot_general x1, matrix products, body(): jnp.dot(collected.reshape(rows_here, span * BLOCK), ladder_ints, precisio...  12 us
    unnamed x12, local copies, waits for them, and re-layouts  11.9 us
    dot_general x1, matrix products, body(): jnp.einsum('rn,onx->orx', onehot, piece, precision=lax.Precision.HIGHEST)  8.53 us
  transfers between devices with their start and end apart: 2, of which 2 were waited for; matrix products, arithmetic and copies ran while one was open for 6% of the time, Pallas kernels for 0%

commit v1 on v0

v1 whole, which is shorter than its diff:
```python
import functools

import jax
import jax.numpy as jnp
from jax import lax
from jax.experimental import pallas as pl
from jax.experimental.pallas import tpu as pltpu
from jax.sharding import PartitionSpec as P

BLOCK = 128
PLANE = 4
CHUNKS = 4
MESH = pl.DeviceIdType.MESH
F32 = jnp.float32
BF16 = jnp.bfloat16


def split(value):
    high = value.astype(BF16)
    return high, (value - high.astype(F32)).astype(BF16)


def loop(count, step, unroll=True):
    def run(index, carry):
        step(index)
        return carry

    lax.fori_loop(0, count, run, 0, unroll=unroll)


def kernel(
    cfg,
    sizes,
    perm,
    shifts,
    amp,
    ladder,
    extra,
    out,
    starts,
    cols,
    tab1,
    tab2,
    tab3,
    tab4,
    tab5,
    tab6,
    raw,
    w_high,
    w_low,
    ladder_sem,
    sems,
    *chunk_refs,
):
    n, per, span, plane, planes, cap, chunks, rows, with_hole = cfg
    rc = rows // chunks
    me = lax.axis_index("vir")
    my_z, my_g = me // plane, me % plane
    bufs = [chunk_refs[k * 10 : (k + 1) * 10] for k in range(chunks)]

    fetch = pltpu.make_async_copy(ladder, raw, ladder_sem)
    fetch.start()

    barrier = pltpu.get_barrier_semaphore()
    z_peers = [((my_z + d) % planes) * plane + my_g for d in range(planes)]
    g_peers = [my_z * plane + (my_g + e) % plane for e in range(plane)]
    peers = z_peers[1:] + g_peers[1:]
    for peer in peers:
        pl.semaphore_signal(barrier, inc=1, device_id={"vir": peer}, device_id_type=MESH)

    def prefix(j, total):
        starts[j] = total
        return total + sizes[j]

    starts[n] = lax.fori_loop(0, n, prefix, jnp.int32(0), unroll=True)

    def find_column(p):
        found = jnp.int32(0)
        for c in range(n):
            found = found + jnp.where(perm[c] == p, c, 0)
        cols[p] = found

    loop(n, find_column, unroll=False)

    def first_slot(start, col):
        return start + (col - start + n * per) % n

    my_col, my_shift = cols[me], shifts[me]
    my_start, my_size = starts[me], sizes[me]
    plane_start = starts[my_z * plane]

    def fill1(q):
        t = first_slot(starts[(q // cap) * plane], my_col) + n * (q % cap)
        tab1[q] = (t // n + my_shift) % per

    loop(planes * cap, fill1)

    def pack1(k):
        s1, r1, own = bufs[k][0], bufs[k][1], bufs[k][9]
        for b in range(per):
            own[b] = amp[k * rc : (k + 1) * rc, b * BLOCK : (b + 1) * BLOCK]
        for d in range(planes):
            z = (my_z + d) % planes
            for i in range(cap):
                block = own[tab1[z * cap + i]]
                if d == 0:
                    r1[my_z * cap + i] = block
                else:
                    s1[d * cap + i] = block

    def z_copy(stage, k, d, src, dst):
        return pltpu.make_async_remote_copy(
            src_ref=src.at[pl.ds(d * cap, cap)],
            dst_ref=dst.at[pl.ds(my_z * cap, cap)],
            send_sem=sems.at[stage, 0, k, d],
            recv_sem=sems.at[stage, 1, k, d],
            device_id={"vir": z_peers[d]},
            device_id_type=MESH,
        )

    def g_copy(stage, k, e, src, dst):
        return pltpu.make_async_remote_copy(
            src_ref=src.at[pl.ds(e * planes, planes)],
            dst_ref=dst.at[pl.ds(my_g * planes, planes)],
            send_sem=sems.at[stage, 0, k, e],
            recv_sem=sems.at[stage, 1, k, e],
            device_id={"vir": g_peers[e]},
            device_id_type=MESH,
        )

    order = sorted(range(1, planes), key=lambda d: abs(d - planes / 2))
    started = []

    def send_z(stage, k, src, dst):
        for d in order:
            copy = z_copy(stage, k, d, src, dst)
            copy.start()
            started.append(copy)

    def send_g(stage, k, src, dst):
        for e in range(1, plane):
            copy = g_copy(stage, k, e, src, dst)
            copy.start()
            started.append(copy)

    def wait_z(stage, k, src, dst):
        for d in range(1, planes):
            z_copy(stage, k, d, src, dst).wait_recv()

    def wait_g(stage, k, src, dst):
        for e in range(1, plane):
            g_copy(stage, k, e, src, dst).wait_recv()

    pack1(0)
    pl.semaphore_wait(barrier, len(peers))
    send_z(0, 0, bufs[0][0], bufs[0][1])
    for k in range(1, chunks):
        pack1(k)
        send_z(0, k, bufs[k][0], bufs[k][1])

    def fill2(q):
        z, j = q // plane, my_z * plane + q % plane
        col = cols[z * plane + my_g]
        t = first_slot(starts[j], col)
        i = (t - first_slot(plane_start, col)) // n
        tab2[q] = z * cap + jnp.minimum(i, cap - 1)

    loop(planes * plane, fill2)

    def fill3(r):
        owner = perm[(my_start + r) % n]
        place = (owner % plane) * planes + owner // plane
        tab3[r] = jnp.where(r < my_size, place, n)

    loop(span, fill3)

    def fill4(q):
        g, z = q // planes, q % planes
        r = (cols[z * plane + g] - my_start + n * per) % n
        tab4[q] = jnp.minimum(r, span - 1)

    loop(planes * plane, fill4)

    def fill5(q):
        z, i = q // cap, q % cap
        t = first_slot(plane_start, cols[z * plane + my_g]) + n * i
        j = jnp.int32(0)
        for step in range(plane - 1):
            j = j + jnp.where(starts[my_z * plane + step + 1] <= t, 1, 0)
        tab5[q] = j * planes + z

    loop(planes * cap, fill5)

    def fill6(b):
        t = ((b + per - my_shift) % per) * n + my_col
        z = jnp.int32(0)
        for step in range(1, planes):
            z = z + jnp.where(starts[step * plane] <= t, 1, 0)
        i = (t - first_slot(starts[z * plane], my_col)) // n
        tab6[b] = z * cap + jnp.minimum(i, cap - 1)

    loop(per, fill6)

    wide = 2 * BLOCK
    if with_hole:
        h_high, h_low = split(extra[...])
        h_both = jnp.concatenate([h_high, h_low], axis=0)

        def hole_tile(c):
            at = pl.ds(pl.multiple_of(c * wide, wide), wide)
            a_high, a_low = split(amp[:, at])
            both = jnp.dot(h_both, a_high, preferred_element_type=F32)
            cross = jnp.dot(h_high, a_low, preferred_element_type=F32)
            out[:, at] = both[:rows] + (both[rows:] + cross)

        loop(per * BLOCK // wide, hole_tile, unroll=False)
    else:
        out[...] = extra[...]

    fetch.wait()
    part = 64

    def split_rows(i):
        at = pl.ds(pl.multiple_of(i * part, part), part)
        high, low = split(raw[at, :])
        w_high[at, :] = high
        w_low[at, :] = low

    loop(span * BLOCK // part, split_rows, unroll=False)

    def stage_a(k):
        s1, r1, s2, r2 = bufs[k][:4]
        wait_z(0, k, s1, r1)
        for e in range(plane):
            j = (my_g + e) % plane
            for z in range(planes):
                block = r1[tab2[z * plane + j]]
                if e == 0:
                    r2[my_g * planes + z] = block
                else:
                    s2[e * planes + z] = block
        send_g(1, k, s2, r2)

    def stage_b(k):
        s2, r2, both, prod, s3, r3 = bufs[k][2:8]
        wait_g(1, k, s2, r2)
        r2[n] = jnp.zeros((rc, BLOCK), F32)
        for r in range(span):
            high, low = split(r2[tab3[r]])
            both[:rc, r * BLOCK : (r + 1) * BLOCK] = high
            both[rc:, r * BLOCK : (r + 1) * BLOCK] = low

        def tile(c):
            at = pl.ds(pl.multiple_of(c * wide, wide), wide)
            main = jnp.dot(both[...], w_high[:, at], preferred_element_type=F32)
            cross = jnp.dot(both[:rc], w_low[:, at], preferred_element_type=F32)
            total = main[:rc] + (main[rc:] + cross)
            for half in range(wide // BLOCK):
                prod[c * (wide // BLOCK) + half] = total[:, half * BLOCK : (half + 1) * BLOCK]

        loop(span * BLOCK // wide, tile, unroll=False)
        for e in range(plane):
            g = (my_g + e) % plane
            for z in range(planes):
                block = prod[tab4[g * planes + z]]
                if e == 0:
                    r3[my_g * planes + z] = block
                else:
                    s3[e * planes + z] = block
        send_g(2, k, s3, r3)

    def stage_c(k):
        s3, r3, r4 = bufs[k][6:9]
        s4 = bufs[k][0]
        wait_g(2, k, s3, r3)
        for d in order:
            z_copy(0, k, d, bufs[k][0], bufs[k][1]).wait_send()
        for d in range(planes):
            z = (my_z + d) % planes
            for i in range(cap):
                block = r3[tab5[z * cap + i]]
                if d == 0:
                    r4[my_z * cap + i] = block
                else:
                    s4[d * cap + i] = block
        send_z(3, k, s4, r4)

    def stage_d(k):
        r4 = bufs[k][8]
        wait_z(3, k, bufs[k][0], r4)
        for b in range(per):
            block = r4[tab6[b]]
            at = (slice(k * rc, (k + 1) * rc), slice(b * BLOCK, (b + 1) * BLOCK))
            out[at] = out[at] + block

    for step in range(chunks + 2):
        if step < chunks:
            stage_a(step)
        if 0 <= step - 1 < chunks:
            stage_b(step - 1)
        if 0 <= step - 2 < chunks:
            stage_c(step - 2)
    for k in range(chunks):
        stage_d(k)
    for k in range(chunks):
        for e in range(1, plane):
            g_copy(1, k, e, bufs[k][2], bufs[k][3]).wait_send()
            g_copy(2, k, e, bufs[k][6], bufs[k][7]).wait_send()
        for d in order:
            z_copy(3, k, d, bufs[k][0], bufs[k][8]).wait_send()


def ladder_call(amplitudes, ladder_ints, extra, sizes, perm, shifts, with_hole):
    n = lax.axis_size("vir")
    rows, width = amplitudes.shape
    per, span = width // BLOCK, ladder_ints.shape[0] // BLOCK
    plane = PLANE if n % PLANE == 0 else 1
    planes = n // plane
    cap = min(per, -(-plane * span // n))
    chunks = CHUNKS if rows % (16 * CHUNKS) == 0 else 1
    rc = rows // chunks
    cfg = (n, per, span, plane, planes, cap, chunks, rows, with_hole)
    blocks = lambda count: pltpu.VMEM((count, rc, BLOCK), F32)
    chunk_scratch = [
        blocks(planes * cap),
        blocks(planes * cap),
        blocks(n),
        blocks(n + 1),
        pltpu.VMEM((2 * rc, span * BLOCK), BF16),
        blocks(span),
        blocks(n),
        blocks(n),
        blocks(planes * cap),
        blocks(per),
    ]
    smem = pl.BlockSpec(memory_space=pltpu.SMEM)
    vmem = pl.BlockSpec(memory_space=pltpu.VMEM)
    table = lambda count: pltpu.SMEM((count,), jnp.int32)
    return pl.pallas_call(
        functools.partial(kernel, cfg),
        out_shape=jax.ShapeDtypeStruct((rows, width), F32),
        in_specs=[smem, smem, smem, vmem, pl.BlockSpec(memory_space=pl.ANY), vmem],
        out_specs=vmem,
        scratch_shapes=[
            table(n + 1),
            table(n),
            table(planes * cap),
            table(n),
            table(span),
            table(n),
            table(planes * cap),
            table(per),
            pltpu.VMEM(ladder_ints.shape, F32),
            pltpu.VMEM(ladder_ints.shape, BF16),
            pltpu.VMEM(ladder_ints.shape, BF16),
            pltpu.SemaphoreType.DMA,
            pltpu.SemaphoreType.DMA((4, 2, chunks, max(plane, planes))),
            *(chunk_scratch * chunks),
        ],
        compiler_params=pltpu.CompilerParams(
            collective_id=0, has_side_effects=True, vmem_limit_bytes=52 * 2**20
        ),
        cost_estimate=pl.CostEstimate(
            flops=6 * rows * (span * BLOCK) ** 2,
            bytes_accessed=4 * (span * BLOCK) ** 2,
            transcendentals=0,
        ),
    )(sizes, perm, shifts, amplitudes, ladder_ints, extra)


def body(amplitudes, ladder_ints, hole_ints, sector_sizes, device_perm, block_shift):
    with_hole = lax.axis_size("occ") == 1
    if with_hole:
        extra = hole_ints
    else:
        partial_sum = jnp.dot(hole_ints, amplitudes, precision=lax.Precision.HIGHEST)
        extra = lax.psum_scatter(partial_sum, "occ", scatter_dimension=0, tiled=True)
    return ladder_call(
        amplitudes, ladder_ints, extra, sector_sizes, device_perm, block_shift, with_hole
    )


def solution(mesh):
    in_specs = (P(("mol", "occ"), "vir"), P(("mol", "vir"), None), P("mol", "occ"), P(), P(), P())
    out_specs = P(("mol", "occ"), "vir")
    return jax.shard_map(body, mesh=mesh, in_specs=in_specs, out_specs=out_specs, check_vma=False)
```

time: 188 us -> 68.1 us (0.36); the launches traced: 184 us -> 67.1 us
  waiting for transfers between devices: 128 us -> 0 us
  Pallas kernels: 0 us -> 62.2 us
  matrix products: 22.4 us -> 0 us
  between operations: 13.5 us -> 0.01 us
  local copies, waits for them, and re-layouts: 13.4 us -> 4.91 us
  starting transfers between devices: 3.71 us -> 0 us
  other arithmetic: 2.37 us -> 0 us
    all_gather x1 -> x0, waiting for transfers between devices: 96.8 us -> none  [body(): piece = lax.all_gather(blocks, 'vir', axis=1, tiled=True)]
    pallas_call x0 -> x1, Pallas kernels: none -> 62.2 us  [ladder_call(): pl.pallas_call(functools.partial(kernel, cfg), out_shape=jax.ShapeDtypeSt...]
    all_to_all x1 -> x0, waiting for transfers between devices: 31.7 us -> none  [send_back(): lax.all_to_all(outgoing, 'vir', split_axis=1, concat_axis=1, tiled=True)]
    dot_general x4 -> x0, matrix products: 22.4 us -> none  [the longest x1 12 us: body(): jnp.dot(collected.reshape(rows_here, span * BLOCK), ladder_ints, precisio...]
    unnamed x12 -> x11, local copies, waits for them, and re-layouts: 11.9 us -> 4.91 us
    all_to_all x1 -> x0, starting transfers between devices: 3.71 us -> none  [send_back(): lax.all_to_all(outgoing, 'vir', split_axis=1, concat_axis=1, tiled=True)]
  transfers between devices with their start and end apart: 2 -> 0, of which waited for: 2 -> 0; matrix products, arithmetic and copies ran while one was open for 6% -> 0% of each run, Pallas kernels for 0% -> 0%
where the time goes in v1:
time: 68.1 us; the launch traced here: 67.1 us
  Pallas kernels  62.2 us (91%)
  local copies, waits for them, and re-layouts  4.91 us (7%)
    pallas_call x1, Pallas kernels, ladder_call(): pl.pallas_call(functools.partial(kernel, cfg), out_shape=jax.ShapeDtypeSt...  62.2 us
    unnamed x11, local copies, waits for them, and re-layouts  4.91 us

profile of v1, /device:TPU:0, one launch (start us, length us, event | category | flops | bytes accessed | tf_op | source)
XLA Modules:
  0.0 67.1 jit_solution(10187047831369228064)
XLA Ops:
  0.0 0.0 copy-start
  0.0 1.1 %copy-done = f32[192,1024]{1,0:T(8,128)S(1)} copy-done((f32[192,1024]{1,0:T(8,128)S(1)}, f32[192,1024]{1,0:T(8,128)}, u32[]{:S(2)}) %copy-start) | copy-done | bytes 786456
  1.1 0.0 copy-start.1
  1.1 0.9 %copy-done.1 = f32[192,192]{1,0:T(8,128)S(1)} copy-done((f32[192,192]{1,0:T(8,128)S(1)}, f32[192,192]{1,0:T(8,128)}, u32[]{:S(2)}) %copy-start.1) | copy-done | bytes 147480
  2.1 0.0 copy-start.2
  2.1 0.7 copy-done.2
  2.7 0.0 copy-start.3
  2.7 0.7 copy-done.3
  3.4 0.0 copy-start.4
  3.4 0.7 copy-done.4
  4.0 62.2 %shard_map.64 = f32[192,1024]{1,0:T(8,128)S(1)} custom-call(s32[16]{0:T(128)S(1)} %copy-done.2, s32[16]{0:T(128)S(1)} %copy-done.3, s32[16]{0:T(128)S(1)} %copy-done.4, f32[192,1024]{1,0:T(8,128)S(1)} %copy-done, f32[1536,1536]{1,0:T(8,128)} %ladder.1, f32[192,192]{1,0:T(8,128)S(1)} %copy-done.1), custom_call_target="tpu_custom_call" | custom-call | flops 2717908992 | bytes 9437184 | tf_op jit(solution)/shard_map/pallas_call | solution.py:339
  66.3 0.9 %copy.8 = f32[192,1024]{1,0:T(8,128)} copy(f32[192,1024]{1,0:T(8,128)S(1)} %shard_map.64) | data formatting | bytes 1572864
Async XLA Ops:
  0.0 1.1 %copy-start = (f32[192,1024]{1,0:T(8,128)S(1)}, f32[192,1024]{1,0:T(8,128)}, u32[]{:S(2)}) copy-start(f32[192,1024]{1,0:T(8,128)} %amp.1) | copy-start | bytes 2359300
  1.1 0.9 %copy-start.1 = (f32[192,192]{1,0:T(8,128)S(1)}, f32[192,192]{1,0:T(8,128)}, u32[]{:S(2)}) copy-start(f32[192,192]{1,0:T(8,128)} %extra.1) | copy-start | bytes 442372
  2.1 0.7 copy-start.2
  2.7 0.7 copy-start.3
  3.4 0.7 copy-start.4

commit v2 on v1

--- a/solution.py
+++ b/solution.py
@@ -10,6 +10,9 @@
 BLOCK = 128
 PLANE = 4
 CHUNKS = 4
+AHEAD = 1
+CAP = 3
+ORDER = "abc"
 MESH = pl.DeviceIdType.MESH
 F32 = jnp.float32
 BF16 = jnp.bfloat16
@@ -30,13 +33,18 @@
 
 def kernel(
     cfg,
+    sizes_hbm,
+    perm_hbm,
+    shifts_hbm,
+    amp_hbm,
+    ladder,
+    extra_hbm,
+    out,
     sizes,
     perm,
     shifts,
     amp,
-    ladder,
     extra,
-    out,
     starts,
     cols,
     tab1,
@@ -48,7 +56,7 @@
     raw,
     w_high,
     w_low,
-    ladder_sem,
+    load_sems,
     sems,
     *chunk_refs,
 ):
@@ -58,9 +66,6 @@
     my_z, my_g = me // plane, me % plane
     bufs = [chunk_refs[k * 10 : (k + 1) * 10] for k in range(chunks)]
 
-    fetch = pltpu.make_async_copy(ladder, raw, ladder_sem)
-    fetch.start()
-
     barrier = pltpu.get_barrier_semaphore()
     z_peers = [((my_z + d) % planes) * plane + my_g for d in range(planes)]
     g_peers = [my_z * plane + (my_g + e) % plane for e in range(plane)]
@@ -68,24 +73,41 @@
     for peer in peers:
         pl.semaphore_signal(barrier, inc=1, device_id={"vir": peer}, device_id_type=MESH)
 
+    pairs = [
+        (sizes_hbm, sizes),
+        (perm_hbm, perm),
+        (shifts_hbm, shifts),
+        (amp_hbm, amp),
+        (extra_hbm, extra),
+        (ladder, raw),
+    ]
+    loads = [
+        pltpu.make_async_copy(src, dst, load_sems.at[i]) for i, (src, dst) in enumerate(pairs)
+    ]
+    for load in loads:
+        load.start()
+    for load in loads[:3]:
+        load.wait()
+
     def prefix(j, total):
         starts[j] = total
         return total + sizes[j]
 
     starts[n] = lax.fori_loop(0, n, prefix, jnp.int32(0), unroll=True)
 
-    def find_column(p):
+    def column_of(p):
         found = jnp.int32(0)
         for c in range(n):
             found = found + jnp.where(perm[c] == p, c, 0)
-        cols[p] = found
-
-    loop(n, find_column, unroll=False)
+        return found
+
+    def find_column(p):
+        cols[p] = column_of(p)
 
     def first_slot(start, col):
         return start + (col - start + n * per) % n
 
-    my_col, my_shift = cols[me], shifts[me]
+    my_col, my_shift = column_of(me), shifts[me]
     my_start, my_size = starts[me], sizes[me]
     plane_start = starts[my_z * plane]
 
@@ -129,19 +151,14 @@
         )
 
     order = sorted(range(1, planes), key=lambda d: abs(d - planes / 2))
-    started = []
 
     def send_z(stage, k, src, dst):
         for d in order:
-            copy = z_copy(stage, k, d, src, dst)
-            copy.start()
-            started.append(copy)
+            z_copy(stage, k, d, src, dst).start()
 
     def send_g(stage, k, src, dst):
         for e in range(1, plane):
-            copy = g_copy(stage, k, e, src, dst)
-            copy.start()
-            started.append(copy)
+            g_copy(stage, k, e, src, dst).start()
 
     def wait_z(stage, k, src, dst):
         for d in range(1, planes):
@@ -151,12 +168,16 @@
         for e in range(1, plane):
             g_copy(stage, k, e, src, dst).wait_recv()
 
+    loads[3].wait()
     pack1(0)
     pl.semaphore_wait(barrier, len(peers))
     send_z(0, 0, bufs[0][0], bufs[0][1])
     for k in range(1, chunks):
         pack1(k)
-        send_z(0, k, bufs[k][0], bufs[k][1])
+        if k < AHEAD:
+            send_z(0, k, bufs[k][0], bufs[k][1])
+
+    loop(n, find_column, unroll=False)
 
     def fill2(q):
         z, j = q // plane, my_z * plane + q % plane
@@ -202,6 +223,7 @@
     loop(per, fill6)
 
     wide = 2 * BLOCK
+    loads[4].wait()
     if with_hole:
         h_high, h_low = split(extra[...])
         h_both = jnp.concatenate([h_high, h_low], axis=0)
@@ -217,7 +239,7 @@
     else:
         out[...] = extra[...]
 
-    fetch.wait()
+    loads[5].wait()
     part = 64
 
     def split_rows(i):
@@ -293,13 +315,14 @@
             at = (slice(k * rc, (k + 1) * rc), slice(b * BLOCK, (b + 1) * BLOCK))
             out[at] = out[at] + block
 
+    stages = {"a": (0, stage_a), "b": (1, stage_b), "c": (2, stage_c)}
     for step in range(chunks + 2):
-        if step < chunks:
-            stage_a(step)
-        if 0 <= step - 1 < chunks:
-            stage_b(step - 1)
-        if 0 <= step - 2 < chunks:
-            stage_c(step - 2)
+        for name in ORDER:
+            late, stage = stages[name]
+            if 0 <= step - late < chunks:
+                stage(step - late)
+            if name == "a" and AHEAD <= step + AHEAD < chunks:
+                send_z(0, step + AHEAD, bufs[step + AHEAD][0], bufs[step + AHEAD][1])
     for k in range(chunks):
         stage_d(k)
     for k in range(chunks):
@@ -316,7 +339,7 @@
     per, span = width // BLOCK, ladder_ints.shape[0] // BLOCK
     plane = PLANE if n % PLANE == 0 else 1
     planes = n // plane
-    cap = min(per, -(-plane * span // n))
+    cap = min(CAP, per, -(-plane * span // n))
     chunks = CHUNKS if rows % (16 * CHUNKS) == 0 else 1
     rc = rows // chunks
     cfg = (n, per, span, plane, planes, cap, chunks, rows, with_hole)
@@ -333,15 +356,18 @@
         blocks(planes * cap),
         blocks(per),
     ]
-    smem = pl.BlockSpec(memory_space=pltpu.SMEM)
-    vmem = pl.BlockSpec(memory_space=pltpu.VMEM)
     table = lambda count: pltpu.SMEM((count,), jnp.int32)
     return pl.pallas_call(
         functools.partial(kernel, cfg),
         out_shape=jax.ShapeDtypeStruct((rows, width), F32),
-        in_specs=[smem, smem, smem, vmem, pl.BlockSpec(memory_space=pl.ANY), vmem],
-        out_specs=vmem,
+        in_specs=[pl.BlockSpec(memory_space=pl.ANY)] * 6,
+        out_specs=pl.BlockSpec(memory_space=pltpu.VMEM),
         scratch_shapes=[
+            table(n),
+            table(n),
+            table(n),
+            pltpu.VMEM((rows, width), F32),
+            pltpu.VMEM(extra.shape, F32),
             table(n + 1),
             table(n),
             table(planes * cap),
@@ -353,12 +379,12 @@
             pltpu.VMEM(ladder_ints.shape, F32),
             pltpu.VMEM(ladder_ints.shape, BF16),
             pltpu.VMEM(ladder_ints.shape, BF16),
-            pltpu.SemaphoreType.DMA,
+            pltpu.SemaphoreType.DMA((6,)),
             pltpu.SemaphoreType.DMA((4, 2, chunks, max(plane, planes))),
             *(chunk_scratch * chunks),
         ],
         compiler_params=pltpu.CompilerParams(
-            collective_id=0, has_side_effects=True, vmem_limit_bytes=52 * 2**20
+            collective_id=0, has_side_effects=True, vmem_limit_bytes=60 * 2**20
         ),
         cost_estimate=pl.CostEstimate(
             flops=6 * rows * (span * BLOCK) ** 2,

time: 68.1 us -> 62.2 us (0.913); the launches traced: 67.1 us -> 62.1 us
  local copies, waits for them, and re-layouts: 4.91 us -> 2.09 us
  Pallas kernels: 62.2 us -> 60 us
    unnamed x11 -> x1, local copies, waits for them, and re-layouts: 4.91 us -> 2.09 us
    pallas_call x1, Pallas kernels: 62.2 us -> 60 us  [ladder_call(): pl.pallas_call(functools.partial(kernel, cfg), out_shape=jax.ShapeDtypeSt...]
where the time goes in v2:
time: 62.2 us; the launch traced here: 62.1 us
  Pallas kernels  60 us (96%)
  local copies, waits for them, and re-layouts  2.09 us (3%)
    pallas_call x1, Pallas kernels, ladder_call(): pl.pallas_call(functools.partial(kernel, cfg), out_shape=jax.ShapeDtypeSt...  60 us
    unnamed x1, local copies, waits for them, and re-layouts  2.09 us

profile of v2, /device:TPU:0, one launch (start us, length us, event | category | flops | bytes accessed | tf_op | source)
XLA Modules:
  0.0 62.1 jit_solution(5597186835355492349)
XLA Ops:
  0.0 60.0 %shard_map.64 = f32[192,1024]{1,0:T(8,128)} custom-call(s32[16]{0:T(128)} %sizes_hbm.1, s32[16]{0:T(128)} %perm_hbm.1, s32[16]{0:T(128)} %shifts_hbm.1, f32[192,1024]{1,0:T(8,128)} %amp_hbm.1, f32[1536,1536]{1,0:T(8,128)} %ladder.1, f32[192,192]{1,0:T(8,128)} %extra_hbm.1), custom_call_target="tpu_custom_call" | custom-call | flops 2717908992 | bytes 9437184 | tf_op jit(solution)/shard_map/pallas_call | solution.py:360
  60.0 2.1 %copy.8 = f32[192,1024]{1,0:T(8,128)} copy(f32[192,1024]{1,0:T(8,128)} %shard_map.64) | data formatting | bytes 1572864

commit v3 on v2

--- a/solution.py
+++ b/solution.py
@@ -77,10 +77,11 @@
         (sizes_hbm, sizes),
         (perm_hbm, perm),
         (shifts_hbm, shifts),
-        (amp_hbm, amp),
-        (extra_hbm, extra),
-        (ladder, raw),
     ]
+    for k in range(chunks):
+        part = pl.ds(k * rc, rc)
+        pairs.append((amp_hbm.at[part], amp.at[part]))
+    pairs += [(extra_hbm, extra), (ladder, raw)]
     loads = [
         pltpu.make_async_copy(src, dst, load_sems.at[i]) for i, (src, dst) in enumerate(pairs)
     ]
@@ -173,6 +174,7 @@
     pl.semaphore_wait(barrier, len(peers))
     send_z(0, 0, bufs[0][0], bufs[0][1])
     for k in range(1, chunks):
+        loads[3 + k].wait()
         pack1(k)
         if k < AHEAD:
             send_z(0, k, bufs[k][0], bufs[k][1])
@@ -223,7 +225,7 @@
     loop(per, fill6)
 
     wide = 2 * BLOCK
-    loads[4].wait()
+    loads[3 + chunks].wait()
     if with_hole:
         h_high, h_low = split(extra[...])
         h_both = jnp.concatenate([h_high, h_low], axis=0)
@@ -239,7 +241,7 @@
     else:
         out[...] = extra[...]
 
-    loads[5].wait()
+    loads[4 + chunks].wait()
     part = 64
 
     def split_rows(i):
@@ -379,7 +381,7 @@
             pltpu.VMEM(ladder_ints.shape, F32),
             pltpu.VMEM(ladder_ints.shape, BF16),
             pltpu.VMEM(ladder_ints.shape, BF16),
-            pltpu.SemaphoreType.DMA((6,)),
+            pltpu.SemaphoreType.DMA((5 + chunks,)),
             pltpu.SemaphoreType.DMA((4, 2, chunks, max(plane, planes))),
             *(chunk_scratch * chunks),
         ],

time: 62.2 us -> 62.2 us (level)
  no operation moved by 1% of the time
where the time goes in v3:
time: 62.2 us; the launch traced here: 62.1 us
  Pallas kernels  60 us (96%)
  local copies, waits for them, and re-layouts  2.09 us (3%)
    pallas_call x1, Pallas kernels, ladder_call(): pl.pallas_call(functools.partial(kernel, cfg), out_shape=jax.ShapeDtypeSt...  60 us
    unnamed x1, local copies, waits for them, and re-layouts  2.09 us

profile of v3, /device:TPU:0, one launch (start us, length us, event | category | flops | bytes accessed | tf_op | source)
XLA Modules:
  0.0 62.1 jit_solution(2574712720560832383)
XLA Ops:
  0.0 60.0 %shard_map.64 = f32[192,1024]{1,0:T(8,128)} custom-call(s32[16]{0:T(128)} %sizes_hbm.1, s32[16]{0:T(128)} %perm_hbm.1, s32[16]{0:T(128)} %shifts_hbm.1, f32[192,1024]{1,0:T(8,128)} %amp_hbm.1, f32[1536,1536]{1,0:T(8,128)} %ladder.1, f32[192,192]{1,0:T(8,128)} %extra_hbm.1), custom_call_target="tpu_custom_call" | custom-call | flops 2717908992 | bytes 9437184 | tf_op jit(solution)/shard_map/pallas_call | solution.py:362
  60.0 2.1 %copy.8 = f32[192,1024]{1,0:T(8,128)} copy(f32[192,1024]{1,0:T(8,128)} %shard_map.64) | data formatting | bytes 1572864
